TPU v7x, 32 devices: a whole 2x2x4 slice. The times are simulated.
32 devices in a mesh: groups: 2 (over y), layer: 4 (over z), dp: 2 (over x), chan: 2 (over core).
Axes of the slice: x: 2, y: 2, z: 4, core: 2. Of those that a mesh axis runs over, the one named last changes fastest.
Arguments:
- activations: bfloat16 [4, 4, 32, 16, 16, 128], P('layer', None, ('groups', 'dp', 'chan')), parts along dimension 2, may hold values from -0.94921875 to 0.94921875
- weights: bfloat16 [4, 4, 9, 128, 128], P('layer'), may hold values from -0.1875 to 0.1875
- guesses: bfloat16 [4, 32, 16, 16, 128], P('layer', ('groups', 'dp', 'chan')), parts along dimension 1, may hold values from -6 to 6
- terminal: bfloat16 [32, 16, 16, 128], P(('groups', 'dp', 'chan')), parts along dimension 0, may hold values from -6 to 6
- coarse_rates: float32 [4, 128], P('layer'), may hold values from 0.0074 to 1, as said below
- block_layers: int32 [4], P('layer'), may hold values from 1 to 4, 12 in all
Outputs:
- corrected: bfloat16 [4, 32, 16, 16, 128], P('layer', ('groups', 'dp', 'chan')), parts along dimension 1
- kernel_grads: bfloat16 [8, 4, 9, 128, 128], P(('groups', 'layer')), parts along dimension 0
There are 2 independent parts, one for each index of `groups`. A program takes and returns all parts, laid end to end along the dimension named above; an argument that names none is the same for every part. Nothing has to cross between parts.
Inputs may be any that keep to these rules, and one draw needn't show every extreme that they name: `block_layers`: every block holds at least one layer and some block holds exactly 4; the counts sum to 12. `coarse_rates`: strictly positive.
All inputs are finite; a program needn't handle non-finite values.
Results may differ from a plain program's by a relative error of at most 0.0055.
Values may be sent and summed in bfloat16 or wider, within the bound.
A program may use at most 64 MiB of HBM per device.

v0:
```python
import jax
import jax.numpy as jnp
from jax import lax
from jax.sharding import PartitionSpec as P

MMAX = 4
step_size = 0.25
OFFSETS = [(row_off, col_off) for row_off in (-1, 0, 1) for col_off in (-1, 0, 1)]


def shifted(value, axis, steps):
    count = lax.axis_size(axis)
    first, last = (max(0, -steps), min(count, count - steps))
    return lax.ppermute(value, axis, [(source, source + steps) for source in range(first, last)])


def entering(part, axis, combine, identity):
    count = lax.axis_size(axis)
    place = lax.axis_index(axis)
    ahead = count - 1 - place
    gathered = jax.tree.map(lambda a: lax.all_gather(a, axis), part)
    state = jax.tree.map(lambda a, e: jnp.zeros_like(a) + jnp.asarray(e, a.dtype), part, identity)

    def one(turn, state):
        source = count - 1 - turn
        return combine(
            state, jax.tree.map(lambda a: lax.dynamic_index_in_dim(a, source, 0, False), gathered)
        )

    return lax.fori_loop(0, ahead, one, state)


def adjoint_step(adjoint, activation, kernel):
    map_side = adjoint.shape[1]
    rounded = adjoint.astype(jnp.bfloat16)
    padded = jnp.pad(rounded, ((0, 0), (1, 1), (1, 1), (0, 0)))
    summed = jnp.zeros(adjoint.shape, jnp.float32)
    for index, (row_off, col_off) in enumerate(OFFSETS):
        sliced = padded[
            :, 1 - row_off : 1 - row_off + map_side, 1 - col_off : 1 - col_off + map_side, :
        ]
        summed = summed + jnp.dot(sliced, kernel[index].T, preferred_element_type=jnp.float32)
    act_float = activation.astype(jnp.float32)
    return (adjoint + step_size * (1.0 - act_float * act_float) * summed, rounded)


def kernel_grad(activation, rounded):
    map_side = rounded.shape[1]
    padded = jnp.pad(activation, ((0, 0), (1, 1), (1, 1), (0, 0)))
    pieces = []
    for row_off, col_off in OFFSETS:
        sliced = padded[
            :, 1 + row_off : 1 + row_off + map_side, 1 + col_off : 1 + col_off + map_side, :
        ]
        pieces.append(
            lax.dot_general(
                sliced,
                rounded,
                (((0, 1, 2), (0, 1, 2)), ((), ())),
                preferred_element_type=jnp.float32,
            )
        )
    return step_size * jnp.stack(pieces)


def per_device(activations, weights, guesses, terminal, coarse_rates, block_layers):
    layer_count = block_layers[0]
    acts_block = activations[0]
    kernels_block = weights[0]
    at_end = lax.axis_index("layer") == lax.axis_size("layer") - 1
    end_state = terminal.astype(jnp.float32)
    own_guess = guesses[0].astype(jnp.float32)
    received = shifted(guesses, "layer", -1)[0]
    adjoint = jnp.where(at_end, end_state, received.astype(jnp.float32))
    for slot in reversed(range(MMAX)):
        stepped, _ = adjoint_step(adjoint, acts_block[slot], kernels_block[slot])
        adjoint = jnp.where(slot < layer_count, stepped, adjoint)
    residual = adjoint - own_guess
    rates = coarse_rates[0]

    def compose(earlier, later):
        return (later[0] * earlier[0], later[1] + later[0] * earlier[1])

    identity = (jnp.ones_like(rates), jnp.zeros_like(residual))
    _, following = entering((rates, residual), "layer", compose, identity)
    correction = residual + rates * following
    corrected = (own_guess + correction).astype(jnp.bfloat16)
    received = shifted(corrected[None], "layer", -1)[0]
    adjoint = jnp.where(at_end, end_state, received.astype(jnp.float32))
    slot_list = [None] * MMAX
    for slot in reversed(range(MMAX)):
        stepped, rounded = adjoint_step(adjoint, acts_block[slot], kernels_block[slot])
        active = slot < layer_count
        slot_grad = kernel_grad(acts_block[slot], rounded)
        slot_grad = jnp.where(active, slot_grad, jnp.zeros_like(slot_grad))
        slot_list[slot] = slot_grad
        adjoint = jnp.where(active, stepped, adjoint)
    stacked = jnp.stack(slot_list)
    result = lax.psum(stacked, ("dp", "chan")).astype(jnp.bfloat16)
    return (corrected[None], result[None])


def solution(mesh):
    in_specs = (
        P("layer", None, ("groups", "dp", "chan"), None, None, None),
        P("layer", None, None, None, None),
        P("layer", ("groups", "dp", "chan"), None, None, None),
        P(("groups", "dp", "chan"), None, None, None),
        P("layer", None),
        P("layer"),
    )
    out_specs = (
        P("layer", ("groups", "dp", "chan"), None, None, None),
        P(("groups", "layer"), None, None, None, None),
    )
    return jax.shard_map(
        per_device, mesh=mesh, in_specs=in_specs, out_specs=out_specs, check_vma=False
    )
```

profile of v0, /device:TPU:0, one launch (start us, length us, event | category | flops | bytes accessed | tf_op | source)
XLA Modules:
  0.0 162.6 jit_solution(5716062791998601039)
XLA Ops:
  7.2 1.4 collective-permute-start
  9.3 9.5 %collective-permute-done = bf16[1,4,16,16,128]{4,3,2,1,0:T(8,128)(2,1)S(1)} collective-permute-done((bf16[1,4,16,16,128]{4,3,2,1,0:T(8,128)(2,1)}, bf16[1,4,16,16,128]{4,3,2,1,0:T(8,128)(2,1)S(1)}, u32[]{:S(2)}, u32[]{:S(2)}) %collective-permute-start) | collective-permute-done | bytes 262176 | tf_op jit(solution)/shard_map/ppermute | solution.py:14
  18.8 1.0 fusion.60
  19.8 1.0 fusion.63
  22.5 0.7 copy-done
  23.3 0.3 fusion.284
  25.5 0.3 fusion.285
  27.7 0.3 fusion.286
  29.9 0.5 copy-done.4
  30.4 1.1 fusion.12
  31.5 9.3 %all-gather.1 = f32[4,1,128]{2,1,0:T(1,128)S(1)} all-gather(f32[1,1,128]{2,1,0:T(1,128)S(1)} %bitcast.708), channel_id=1, replica_groups=mesh['groups'=2,'layer'=4,'dp'=2,'chan'=2] {'layer'}, dimensions={0}, use_global_device_ids=true | all-gather | bytes 2560 | tf_op jit(solution)/shard_map/all_gather | solution.py:21
  40.9 37.1 %all-gather.4.cloned.1.call-done = f32[16,16,16,128]{3,2,1,0:T(8,128)} async-done(((f32[4,16,16,128]{3,2,1,0:T(8,128)}), f32[16,16,16,128]{3,2,1,0:T(8,128)}) %all-gather.4.cloned.1.call-update) | async-done | bytes 2097168 | tf_op jit(solution)/shard_map/all_gather | solution.py:21
  78.0 3.9 %while.14 = (s32[]{:T(128)}, f32[4,16,16,128]{3,2,1,0:T(8,128)S(1)}, s32[]{:T(128)}, f32[4,4,16,16,128]{4,3,2,1,0:T(8,128)}, f32[4,128]{1,0:T(4,128)S(1)}, /*index=5*/s32[]{:T(128)}, s32[]{:T(128)}, s32[]{:T(128)}, s32[]{:T(128)}) while((s32[]{:T(128)}, f32[4,16,16,128]{3,2,1,0:T(8,128)S(1)}, s32[]{:T(128)}, f32[4,4,16,16,128]{4,3,2,1,0:T(8,128)}, ...), condition=%wide.region_1.2_spmd, body=%wide.region_0.1_spmd.sunk | while | flops 262150 | bytes 1574555 | solution.py:30
  78.1 1.3 bitcast_add_fusion.2
  79.4 1.2 bitcast_add_fusion.2
  80.7 1.2 bitcast_add_fusion.2
  82.0 1.0 fusion.62
  83.0 1.5 collective-permute-start.1
  84.7 8.3 %collective-permute-done.1 = bf16[1,4,16,16,128]{4,3,2,1,0:T(8,128)(2,1)S(1)} collective-permute-done((bf16[1,4,16,16,128]{4,3,2,1,0:T(8,128)(2,1)S(1)}, bf16[1,4,16,16,128]{4,3,2,1,0:T(8,128)(2,1)S(1)}, u32[]{:S(2)}, u32[]{:S(2)}) %collective-permute-start.1) | collective-permute-done | bytes 262176 | tf_op jit(solution)/shard_map/ppermute | solution.py:14
  94.9 0.3 fusion.287
  97.2 0.3 fusion.288
  99.4 0.3 fusion.22
  100.8 0.3 fusion.54
  101.3 0.3 fusion.52
  101.6 0.3 fusion.51
  101.9 0.3 fusion.50
  103.3 0.3 fusion.36
  103.9 0.3 fusion.34
  105.8 0.3 fusion.27
  106.4 0.3 fusion.25
  108.4 0.3 fusion.45
  110.3 45.5 %all-reduce.12 = bf16[4,9,128,128]{3,2,1,0:T(8,128)(2,1)} all-reduce(f32[4,9,128,128]{3,2,1,0:T(8,128)S(1)} %pad_maximum_fusion), channel_id=1, replica_groups=mesh['groups'=2,'layer'=4,'dp'=2,'chan'=2] {'dp','chan'}, use_global_device_ids=true, to_apply=%region_2.3 | all-reduce | flops 589824 | bytes 3538944 | tf_op jit(solution)/shard_map/psum | solution.py:99
  (105 shorter events, 21.0 us)
Async XLA Ops:
  7.2 13.7 %copy-start.3 = (bf16[1,4,9,128,128]{4,3,2,1,0:T(8,128)(2,1)S(1)}, bf16[1,4,9,128,128]{4,3,2,1,0:T(8,128)(2,1)}, u32[]{:S(2)}) copy-start(bf16[1,4,9,128,128]{4,3,2,1,0:T(8,128)(2,1)} %param.9) | copy-start | bytes 3538948
  7.2 70.8 %all-gather.4.cloned.1.call-start = ((), (), s32[]{:S(2)}) async-start(), calls=%async_computation | async-start | bytes 2621440 | tf_op jit(solution)/shard_map/all_gather | solution.py:21
  7.2 11.6 %collective-permute-start = (bf16[1,4,16,16,128]{4,3,2,1,0:T(8,128)(2,1)}, bf16[1,4,16,16,128]{4,3,2,1,0:T(8,128)(2,1)S(1)}, u32[]{:S(2)}, u32[]{:S(2)}) collective-permute-start(bf16[1,4,16,16,128]{4,3,2,1,0:T(8,128)(2,1)} %param.10), channel_id=1, source_target_pairs={{4,0},{8,4},{12,8},{5,1},{9,5},{13,9},{6,2},{10,6},{14,10},{7,3},{... | collective-permute-start | bytes 786440 | tf_op jit(solution)/shard_map/ppermute | solution.py:14
  22.0 1.2 copy-start
  22.0 1.3 copy-start.2
  29.4 1.0 copy-start.4
  30.4 1.1 copy-start.6
  78.0 3.9 %copy-start.1 = (f32[4,16,16,128]{3,2,1,0:T(8,128)S(1)}, f32[4,16,16,128]{3,2,1,0:T(8,128)}, u32[]{:S(2)}) copy-start(f32[4,16,16,128]{3,2,1,0:T(8,128)} %fusion.12) | copy-start | bytes 1572868
  83.0 10.0 %copy-start.5 = (bf16[1,4,16,16,128]{4,3,2,1,0:T(8,128)(2,1)}, bf16[1,4,16,16,128]{4,3,2,1,0:T(8,128)(2,1)S(1)}, u32[]{:S(2)}) copy-start(bf16[1,4,16,16,128]{4,3,2,1,0:T(8,128)(2,1)S(1)} %fusion.62) | copy-start | bytes 786436
  83.0 9.9 %collective-permute-start.1 = (bf16[1,4,16,16,128]{4,3,2,1,0:T(8,128)(2,1)S(1)}, bf16[1,4,16,16,128]{4,3,2,1,0:T(8,128)(2,1)S(1)}, u32[]{:S(2)}, u32[]{:S(2)}) collective-permute-start(bf16[1,4,16,16,128]{4,3,2,1,0:T(8,128)(2,1)S(1)} %fusion.62), channel_id=1, source_target_pairs={{4,0},{8,4},{12,8},{5,1},{9,5},{13,9},{6,2},{10,6},{14,10},{7,3},{... | collective-permute-start | bytes 786440 | tf_op jit(solution)/shard_map/ppermute | solution.py:14
Sparse Core Ops, SparseCore 0:
  31.6 46.3 all-gather.3
where the time goes:
time: 163 us
  waiting for transfers between devices  54.9 us (34%)
  blocking collectives  54.8 us (34%)
  matrix products  26.5 us (16%)
  between operations  15.5 us (10%)
  other arithmetic  6.39 us (4%)
  starting transfers between devices  2.93 us (2%)
    psum x1, blocking collectives, per_device(): result = lax.psum(stacked, ('dp', 'chan')).astype(jnp.bfloat16)  45.5 us
    all_gather x1, waiting for transfers between devices, entering(): gathered = jax.tree.map(lambda a: lax.all_gather(a, axis), part)  37.1 us
    ppermute x2, waiting for transfers between devices, shifted(): lax.ppermute(value, axis, [(source, source + steps) for source in range(f...  17.7 us
    dot_general x63, matrix products, adjoint_step(): jnp.dot(sliced, kernel[index].T, preferred_element_type=jnp.float32)  16.6 us
    dot_general x36, matrix products, kernel_grad(): lax.dot_general(sliced, rounded, (((0, 1, 2), (0, 1, 2)), ((), ())), pref...  9.87 us
    all_gather x1, blocking collectives, entering(): gathered = jax.tree.map(lambda a: lax.all_gather(a, axis), part)  9.34 us
    add x3, other arithmetic, compose(): return (later[0] * earlier[0], later[1] + later[0] * earlier[1])  3.78 us
  transfers between devices with their start and end apart: 3, of which 3 were waited for; matrix products, arithmetic and copies ran while one was open for 0% of the time, Pallas kernels for 0%

commit v1 on v0

--- a/solution.py
+++ b/solution.py
@@ -96,7 +96,7 @@
         slot_list[slot] = slot_grad
         adjoint = jnp.where(active, stepped, adjoint)
     stacked = jnp.stack(slot_list)
-    result = lax.psum(stacked, ("dp", "chan")).astype(jnp.bfloat16)
+    result = lax.psum(lax.psum(stacked, "chan"), "dp").astype(jnp.bfloat16)
     return (corrected[None], result[None])
 
 

time: 163 us -> 200 us (1.23)
  waiting for transfers between devices: 54.9 us -> 74.7 us
  blocking collectives: 54.8 us -> 70.1 us
    psum x0 -> x1, waiting for transfers between devices: none -> 19.9 us  [per_device(): result = lax.psum(lax.psum(stacked, 'chan'), 'dp').astype(jnp.bfloat16)]
    psum x1, blocking collectives: 45.5 us -> 60.8 us  [per_device(): result = lax.psum(lax.psum(stacked, 'chan'), 'dp').astype(jnp.bfloat16)]
  transfers between devices with their start and end apart: 3 -> 4, of which waited for: 3 -> 4; matrix products, arithmetic and copies ran while one was open for 0% -> 0% of each run, Pallas kernels for 0% -> 0%
where the time goes in v1:
time: 200 us; the launch traced here: 199 us
  waiting for transfers between devices  74.7 us (37%)
  blocking collectives  70.1 us (35%)
  matrix products  26.4 us (13%)
  between operations  15.5 us (8%)
  other arithmetic  7.79 us (4%)
  starting transfers between devices  2.98 us (1%)
    psum x1, blocking collectives, per_device(): result = lax.psum(lax.psum(stacked, 'chan'), 'dp').astype(jnp.bfloat16)  60.8 us
    all_gather x1, waiting for transfers between devices, entering(): gathered = jax.tree.map(lambda a: lax.all_gather(a, axis), part)  37.1 us
    psum x1, waiting for transfers between devices, per_device(): result = lax.psum(lax.psum(stacked, 'chan'), 'dp').astype(jnp.bfloat16)  19.9 us
    ppermute x2, waiting for transfers between devices, shifted(): lax.ppermute(value, axis, [(source, source + steps) for source in range(f...  17.7 us
    dot_general x63, matrix products, adjoint_step(): jnp.dot(sliced, kernel[index].T, preferred_element_type=jnp.float32)  16.6 us
    dot_general x36, matrix products, kernel_grad(): lax.dot_general(sliced, rounded, (((0, 1, 2), (0, 1, 2)), ((), ())), pref...  9.8 us
    all_gather x1, blocking collectives, entering(): gathered = jax.tree.map(lambda a: lax.all_gather(a, axis), part)  9.34 us
  transfers between devices with their start and end apart: 4, of which 4 were waited for; matrix products, arithmetic and copies ran while one was open for 0% of the time, Pallas kernels for 0%

profile of v1, /device:TPU:0, one launch (start us, length us, event | category | flops | bytes accessed | tf_op | source)
XLA Modules:
  0.0 199.1 jit_solution(9499280281528511257)
XLA Ops:
  7.2 1.4 collective-permute-start
  9.3 9.5 %collective-permute-done = bf16[1,4,16,16,128]{4,3,2,1,0:T(8,128)(2,1)S(1)} collective-permute-done((bf16[1,4,16,16,128]{4,3,2,1,0:T(8,128)(2,1)}, bf16[1,4,16,16,128]{4,3,2,1,0:T(8,128)(2,1)S(1)}, u32[]{:S(2)}, u32[]{:S(2)}) %collective-permute-start) | collective-permute-done | bytes 262176 | tf_op jit(solution)/shard_map/ppermute | solution.py:14
  18.8 1.0 fusion.60
  19.8 1.0 fusion.63
  22.5 0.7 copy-done
  23.3 0.3 fusion.284
  25.5 0.3 fusion.285
  27.7 0.3 fusion.286
  29.9 0.5 copy-done.4
  30.4 1.1 fusion.12
  31.6 9.3 %all-gather.1 = f32[4,1,128]{2,1,0:T(1,128)S(1)} all-gather(f32[1,1,128]{2,1,0:T(1,128)S(1)} %bitcast.708), channel_id=1, replica_groups=mesh['groups'=2,'layer'=4,'dp'=2,'chan'=2] {'layer'}, dimensions={0}, use_global_device_ids=true | all-gather | bytes 2560 | tf_op jit(solution)/shard_map/all_gather | solution.py:21
  40.9 37.1 %all-gather.4.cloned.1.call-done = f32[16,16,16,128]{3,2,1,0:T(8,128)} async-done(((f32[4,16,16,128]{3,2,1,0:T(8,128)}), f32[16,16,16,128]{3,2,1,0:T(8,128)}) %all-gather.4.cloned.1.call-update) | async-done | bytes 2097168 | tf_op jit(solution)/shard_map/all_gather | solution.py:21
  78.0 3.9 %while.14 = (s32[]{:T(128)}, f32[4,16,16,128]{3,2,1,0:T(8,128)S(1)}, s32[]{:T(128)}, f32[4,4,16,16,128]{4,3,2,1,0:T(8,128)}, f32[4,128]{1,0:T(4,128)S(1)}, /*index=5*/s32[]{:T(128)}, s32[]{:T(128)}, s32[]{:T(128)}, s32[]{:T(128)}) while((s32[]{:T(128)}, f32[4,16,16,128]{3,2,1,0:T(8,128)S(1)}, s32[]{:T(128)}, f32[4,4,16,16,128]{4,3,2,1,0:T(8,128)}, ...), condition=%wide.region_1.2_spmd, body=%wide.region_0.1_spmd.sunk | while | flops 262150 | bytes 1574555 | solution.py:30
  78.1 1.3 bitcast_add_fusion.2
  79.4 1.2 bitcast_add_fusion.2
  80.7 1.2 bitcast_add_fusion.2
  82.0 1.0 fusion.62
  83.0 1.5 collective-permute-start.1
  84.7 8.3 %collective-permute-done.1 = bf16[1,4,16,16,128]{4,3,2,1,0:T(8,128)(2,1)S(1)} collective-permute-done((bf16[1,4,16,16,128]{4,3,2,1,0:T(8,128)(2,1)S(1)}, bf16[1,4,16,16,128]{4,3,2,1,0:T(8,128)(2,1)S(1)}, u32[]{:S(2)}, u32[]{:S(2)}) %collective-permute-start.1) | collective-permute-done | bytes 262176 | tf_op jit(solution)/shard_map/ppermute | solution.py:14
  94.9 0.3 fusion.287
  97.2 0.3 fusion.288
  99.4 0.3 fusion.22
  100.8 0.3 fusion.54
  103.3 0.3 fusion.36
  103.8 0.3 fusion.34
  105.8 0.3 fusion.27
  108.3 0.3 fusion.45
  108.9 0.3 fusion.43
  109.2 0.3 fusion.42
  110.0 1.6 pad_maximum_fusion
  111.6 19.9 %all-reduce.14.cloned.1.call-done = f32[4,9,128,128]{3,2,1,0:T(8,128)} async-done(((f32[4,9,128,128]{3,2,1,0:T(8,128)}), f32[4,9,128,128]{3,2,1,0:T(8,128)}) %all-reduce.14.cloned.1.call-update) | async-done | bytes 2359312 | tf_op jit(solution)/shard_map/psum | solution.py:99
  131.5 60.8 %all-reduce.15 = bf16[4,9,128,128]{3,2,1,0:T(8,128)(2,1)} all-reduce(f32[4,9,128,128]{3,2,1,0:T(8,128)} %all-reduce.14.cloned.1.call-done), channel_id=1, replica_groups=mesh['groups'=2,'layer'=4,'dp'=2,'chan'=2] {'dp'}, use_global_device_ids=true, to_apply=%region_3.4 | all-reduce | flops 589824 | bytes 3538944 | tf_op jit(solution)/shard_map/psum | solution.py:99
  (108 shorter events, 21.3 us)
Async XLA Ops:
  7.2 13.7 %copy-start.3 = (bf16[1,4,9,128,128]{4,3,2,1,0:T(8,128)(2,1)S(1)}, bf16[1,4,9,128,128]{4,3,2,1,0:T(8,128)(2,1)}, u32[]{:S(2)}) copy-start(bf16[1,4,9,128,128]{4,3,2,1,0:T(8,128)(2,1)} %param.9) | copy-start | bytes 3538948
  7.2 70.8 %all-gather.4.cloned.1.call-start = ((), (), s32[]{:S(2)}) async-start(), calls=%async_computation.1 | async-start | bytes 2621440 | tf_op jit(solution)/shard_map/all_gather | solution.py:21
  7.2 11.6 %collective-permute-start = (bf16[1,4,16,16,128]{4,3,2,1,0:T(8,128)(2,1)}, bf16[1,4,16,16,128]{4,3,2,1,0:T(8,128)(2,1)S(1)}, u32[]{:S(2)}, u32[]{:S(2)}) collective-permute-start(bf16[1,4,16,16,128]{4,3,2,1,0:T(8,128)(2,1)} %param.10), channel_id=1, source_target_pairs={{4,0},{8,4},{12,8},{5,1},{9,5},{13,9},{6,2},{10,6},{14,10},{7,3},{... | collective-permute-start | bytes 786440 | tf_op jit(solution)/shard_map/ppermute | solution.py:14
  22.0 1.2 copy-start
  22.0 1.3 copy-start.2
  29.4 1.0 copy-start.4
  30.4 1.2 copy-start.6
  31.5 100.0 %all-reduce.14.cloned.1.call-start = ((), (), s32[]{:S(2)}) async-start(), calls=%async_computation | async-start | bytes 4718592 | tf_op jit(solution)/shard_map/psum | solution.py:99
  78.0 3.9 %copy-start.1 = (f32[4,16,16,128]{3,2,1,0:T(8,128)S(1)}, f32[4,16,16,128]{3,2,1,0:T(8,128)}, u32[]{:S(2)}) copy-start(f32[4,16,16,128]{3,2,1,0:T(8,128)} %fusion.12) | copy-start | bytes 1572868
  83.0 10.0 %copy-start.5 = (bf16[1,4,16,16,128]{4,3,2,1,0:T(8,128)(2,1)}, bf16[1,4,16,16,128]{4,3,2,1,0:T(8,128)(2,1)S(1)}, u32[]{:S(2)}) copy-start(bf16[1,4,16,16,128]{4,3,2,1,0:T(8,128)(2,1)S(1)} %fusion.62) | copy-start | bytes 786436
  83.0 9.9 %collective-permute-start.1 = (bf16[1,4,16,16,128]{4,3,2,1,0:T(8,128)(2,1)S(1)}, bf16[1,4,16,16,128]{4,3,2,1,0:T(8,128)(2,1)S(1)}, u32[]{:S(2)}, u32[]{:S(2)}) collective-permute-start(bf16[1,4,16,16,128]{4,3,2,1,0:T(8,128)(2,1)S(1)} %fusion.62), channel_id=1, source_target_pairs={{4,0},{8,4},{12,8},{5,1},{9,5},{13,9},{6,2},{10,6},{14,10},{7,3},{... | collective-permute-start | bytes 786440 | tf_op jit(solution)/shard_map/ppermute | solution.py:14
Sparse Core Ops, SparseCore 0:
  31.6 46.3 all-gather.3
  111.8 19.7 all-reduce.13
